TPU v7x, 128 devices: a whole 4x4x4 slice. The times are simulated.
128 devices in a mesh: dp: 4 (over x), ctx: 32 (over z, y, core).
Axes of the slice: x: 4, y: 4, z: 4, core: 2. Of those that a mesh axis runs over, the one named last changes fastest.
Arguments:
- queries: bfloat16 [16384, 4096], P(('dp', 'ctx')), parts along dimension 0, may hold values from -8 to 8
- keys: bfloat16 [16384, 512], P(('dp', 'ctx')), parts along dimension 0, may hold values from -8 to 8
- values: bfloat16 [16384, 512], P(('dp', 'ctx')), parts along dimension 0, may hold values from -6 to 6
- grad_out: bfloat16 [16384, 4096], P(('dp', 'ctx')), parts along dimension 0, may hold values from -6 to 6
- lengths: int32 [32], P('dp'), parts along dimension 0, may hold values from 1 to 2048, 4096 in all
- plan: int32 [128], P('dp'), parts along dimension 0, may hold values from 0 to 31, each once
Outputs:
- grad_queries: float32 [16384, 4096], P(('dp', 'ctx')), parts along dimension 0
- grad_keys: float32 [16384, 512], P(('dp', 'ctx')), parts along dimension 0
- grad_values: float32 [16384, 512], P(('dp', 'ctx')), parts along dimension 0
There are 4 independent parts, one for each index of `dp`. A program takes and returns all parts, laid end to end along the dimension named above; each array names one. Nothing has to cross between parts.
Inputs may be any that keep to these rules, and one draw needn't show every extreme that they name: The lengths sum to 4096 and the longest is exactly 2048. `plan`: each query block appears in exactly one slot.
All inputs are finite; a program needn't handle non-finite values.
Results may differ from a plain program's by a relative error of at most 0.024.
Values may be sent and summed in bfloat16 or wider, within the bound.
No kernel may reach another device: no remote copies, remote signals or barrier semaphores. Data moves between devices by JAX's collectives and lax.ppermute only.
A program may use at most 128 MiB of HBM per device.

v0:
```python
import functools
import math

import jax
import jax.numpy as jnp
from jax import lax
from jax.experimental import pallas as pl
from jax.experimental.pallas import tpu as pltpu
from jax.sharding import PartitionSpec as P

HD = 128
BLOCK = 128
DOCS = 8
KVH = 4
GROUP = 8
NZ = 4
NY = 4
SEQ = 4096
NBLK = 32
WIDTH = GROUP * HD
TILE = 256
MAXTILES = 9
SIZES = (2, 1)
PAIR = 256
PAIRS = WIDTH // PAIR
NEG = -1e30
INV_ROOT = 1.0 / math.sqrt(HD)
EXP_SCALE = INV_ROOT / math.log(2.0)


SMEM = pl.BlockSpec(memory_space=pltpu.SMEM)
VMEM = pl.BlockSpec(memory_space=pltpu.VMEM)
HBM = pl.BlockSpec(memory_space=pltpu.HBM)
SMALL_VMEM_BYTES = 12 * 1024 * 1024
PACK_VMEM_BYTES = 56 * 1024 * 1024
VMEM_BYTES = 40 * 1024 * 1024
BLOCK_FLOPS = 5 * 2 * WIDTH * 1024 * HD


def cost(flops, nbytes):
    return pl.CostEstimate(flops=flops, bytes_accessed=nbytes, transcendentals=0)


def ring(dz, dy, dc):
    return [
        ((z * NY + y) * 2 + c, ((z + dz) % NZ * NY + (y + dy) % NY) * 2 + (c ^ dc))
        for z in range(NZ)
        for y in range(NY)
        for c in range(2)
    ]


SAME_CORE = [[chip * 2 + core for chip in range(NZ * NY)] for core in range(2)]


def exchange(x):
    return lax.all_to_all(
        x, "ctx", split_axis=0, concat_axis=0, axis_index_groups=SAME_CORE, tiled=True
    )


def send(x, dz, dy, dc):
    return lax.ppermute(x, "ctx", ring(dz, dy, dc))


def at_head(place, d, width):
    return pl.ds(pl.multiple_of((place[0] + d + NZ) % NZ * width, width), width)


def here():
    me = lax.axis_index("ctx")
    return lax.shift_right_logical(me, 3), lax.shift_right_logical(me, 1) & 3, me & 1


def pack_kernel(width, left, right, *refs):
    outs, sems = refs[:NZ], refs[NZ]
    place = here()
    copies = []
    for d, out in enumerate(outs):
        for half, source in enumerate((left, right)):
            copies.append(pltpu.make_async_copy(
                source.at[:, at_head(place, d, width)],
                out.at[:, half * width:(half + 1) * width],
                sems.at[len(copies)],
            ))
            copies[-1].start()
    for copy in copies:
        copy.wait()


def pack(left, right):
    width = left.shape[1] // KVH
    return pl.pallas_call(
        functools.partial(pack_kernel, width),
        out_shape=[jax.ShapeDtypeStruct((BLOCK, 2 * width), left.dtype)] * NZ,
        in_specs=[HBM] * 2,
        out_specs=[VMEM] * NZ,
        scratch_shapes=[pltpu.SemaphoreType.DMA((2 * NZ,))],
        compiler_params=pltpu.CompilerParams(vmem_limit_bytes=PACK_VMEM_BYTES),
        cost_estimate=cost(0, 4 * left.size * 2),
        name="pack",
    )(left, right)


def put_heads(place, parts, out, wide, sems):
    copies = []
    for i, (d, part) in enumerate(parts):
        wide[i] = part[...].astype(wide.dtype)
        copies.append(
            pltpu.make_async_copy(wide.at[i], out.at[:, at_head(place, d, WIDTH)], sems.at[i])
        )
        copies[-1].start()
    return copies


def join_near_kernel(dq0, dq1, dq3, out, wide, sems):
    for copy in put_heads(here(), ((0, dq0), (1, dq1), (3, dq3)), out, wide, sems):
        copy.wait()


def join_near(dq0, dq1, dq3):
    return pl.pallas_call(
        join_near_kernel,
        out_shape=jax.ShapeDtypeStruct((BLOCK, KVH * WIDTH), jnp.float32),
        in_specs=[VMEM] * 3,
        out_specs=HBM,
        scratch_shapes=[
            pltpu.VMEM((3, BLOCK, WIDTH), jnp.float32),
            pltpu.SemaphoreType.DMA((3,)),
        ],
        compiler_params=pltpu.CompilerParams(vmem_limit_bytes=SMALL_VMEM_BYTES),
        cost_estimate=cost(0, BLOCK * KVH * WIDTH * 6),
        name="join_near",
    )(dq0, dq1, dq3)


def finish_kernel(partials, dq2, grad_in, out, dk, dv, wide, sems):
    copies = put_heads(here(), ((2, dq2),), out, wide, sems)
    for h in range(KVH):
        total = partials[h * NY].astype(jnp.float32)
        for y in range(1, NY):
            total = total + partials[h * NY + y].astype(jnp.float32)
        dk[:, h * HD:(h + 1) * HD] = total[:, :HD]
        dv[:, h * HD:(h + 1) * HD] = total[:, HD:]
    for copy in copies:
        copy.wait()


def finish(partials, dq2, grad_query):
    return pl.pallas_call(
        finish_kernel,
        out_shape=[jax.ShapeDtypeStruct((BLOCK, KVH * WIDTH), jnp.float32)]
        + [jax.ShapeDtypeStruct((BLOCK, KVH * HD), jnp.float32)] * 2,
        in_specs=[VMEM, VMEM, HBM],
        out_specs=[HBM, VMEM, VMEM],
        input_output_aliases={2: 0},
        scratch_shapes=[
            pltpu.VMEM((1, BLOCK, WIDTH), jnp.float32),
            pltpu.SemaphoreType.DMA((1,)),
        ],
        compiler_params=pltpu.CompilerParams(vmem_limit_bytes=SMALL_VMEM_BYTES),
        cost_estimate=cost(0, 4 * 2**20),
        name="finish",
    )(partials, dq2, grad_query)


def slots(place):
    for core_rel in range(2):
        for chip in range(NZ * NY):
            slot = chip * 2 + (place[2] ^ core_rel)
            yield core_rel, chip, pl.ds(pl.multiple_of(slot * BLOCK, BLOCK), BLOCK)


def attend(
    place, plan, lengths, distances, qds, dqs,
    keys, values, dkeys, dvalues, scores, probs, qs, qst, gs, gst, dqt,
):
    z, y, c = place[0], place[1], place[2]

    def block(i, carry):
        d = jnp.int32(distances[0])
        for k, qd in enumerate(qds):
            d = jnp.where(i == k, distances[k], d)

            @pl.when(i == k)
            def _(qd=qd):
                for g in range(GROUP):
                    rows = slice(g * BLOCK, (g + 1) * BLOCK)
                    q = qd[:, g * HD:(g + 1) * HD]
                    o = qd[:, WIDTH + g * HD:WIDTH + (g + 1) * HD]
                    qs[rows, :] = q
                    gs[rows, :] = o
                    qst[:, rows] = q.T
                    gst[:, rows] = o.T

        first = plan[((z - d + NZ) % NZ * NY + y) * 2 + c] * BLOCK
        pos = first + lax.broadcasted_iota(jnp.int32, (1, BLOCK), 1)
        start = jnp.zeros((1, BLOCK), jnp.int32)
        low = jnp.int32(0)
        end = jnp.int32(0)
        for e in range(DOCS):
            end = end + lengths[e]
            start = jnp.where(end <= pos, end, start)
            low = jnp.where(end <= first, end, low)
        tiles = (first + BLOCK - low // BLOCK * BLOCK + TILE - 1) // TILE
        base = jnp.maximum(first + BLOCK - tiles * TILE, 0)

        def sweep(body, state):
            done = jnp.int32(0)
            for size in SIZES:
                count = (tiles - done) // size
                state = lax.fori_loop(
                    0,
                    count,
                    lambda t, state, done=done, size=size: body(
                        (done + t * size) * TILE, size * TILE, state
                    ),
                    state,
                )
                done = done + count * size
            return state

        def stat(offset, size, state):
            offset = pl.multiple_of(offset, TILE)
            rows = pl.ds(pl.multiple_of(base + offset, BLOCK), size)
            key_pos = base + offset + lax.broadcasted_iota(jnp.int32, (size, BLOCK), 0)
            allowed = (key_pos >= start) & (key_pos <= pos)
            allowed = jnp.concatenate([allowed] * (PAIR // BLOCK), axis=1)
            k, v = keys[rows, :], values[rows, :]
            result = []

            def fold(x, op):
                x = x.reshape(-1, 8, PAIR)
                out = x[0]
                for i in range(1, x.shape[0]):
                    out = op(out, x[i])
                return out

            def dots(p):
                cols = slice(p * PAIR, (p + 1) * PAIR)
                high = None
                for r in range(0, size, TILE):
                    at = pl.ds(offset + r, TILE)
                    s = jnp.dot(k[r:r + TILE], qst[:, cols], preferred_element_type=jnp.float32)
                    s = jnp.where(allowed[r:r + TILE], s * EXP_SCALE, NEG)
                    scores[at, cols] = s
                    here_high = fold(s, jnp.maximum)
                    high = here_high if high is None else jnp.maximum(high, here_high)
                    probs[at, cols] = jnp.dot(v[r:r + TILE], gst[:, cols], preferred_element_type=jnp.float32)
                return high

            def sums(p, high):
                cols = slice(p * PAIR, (p + 1) * PAIR)
                top, total, dot = state[p]
                new_top = jnp.maximum(top, jnp.max(high, axis=0, keepdims=True))
                factor = jnp.exp2(top - new_top)
                add, mul = jnp.zeros((8, PAIR), jnp.float32), jnp.zeros((8, PAIR), jnp.float32)
                for r in range(0, size, TILE):
                    at = pl.ds(offset + r, TILE)
                    e = jnp.exp2(scores[at, cols] - new_top)
                    add = add + fold(e, jnp.add)
                    mul = mul + fold(e * probs[at, cols], jnp.add)
                result.append((
                    new_top,
                    total * factor + jnp.sum(add, axis=0, keepdims=True),
                    dot * factor + jnp.sum(mul, axis=0, keepdims=True),
                ))

            ahead = [dots(p) for p in range(1)]
            for p in range(PAIRS):
                if p + 1 < PAIRS:
                    ahead.append(dots(p + 1))
                sums(p, ahead[p])
            return tuple(result)

        zero = jnp.zeros((1, PAIR), jnp.float32)
        state = sweep(stat, ((jnp.full((1, PAIR), NEG, jnp.float32), zero, zero),) * PAIRS)
        norms = [(top + jnp.log2(total), dot / total) for top, total, dot in state]
        dqt[...] = jnp.zeros((HD, WIDTH), jnp.float32)

        def grad(offset, size, carry):
            offset = pl.multiple_of(offset, TILE)
            rows = pl.ds(pl.multiple_of(base + offset, BLOCK), size)
            at = pl.ds(offset, size)
            kt = keys[rows, :].T
            dk = dkeys[rows, :]
            dv = dvalues[rows, :]
            for p in range(PAIRS):
                cols = slice(p * PAIR, (p + 1) * PAIR)
                log_norm, row_dot = norms[p]
                prob = jnp.exp2(scores[at, cols] - log_norm)
                ds = prob * (probs[at, cols] - row_dot)
                prob = prob.astype(jnp.bfloat16)
                ds = ds.astype(jnp.bfloat16)
                dv = dv + jnp.dot(prob, gs[cols, :], preferred_element_type=jnp.float32)
                dk = dk + jnp.dot(ds, qs[cols, :], preferred_element_type=jnp.float32)
                dqt[:, cols] += jnp.dot(kt, ds, preferred_element_type=jnp.float32)
            dkeys[rows, :] = dk
            dvalues[rows, :] = dv
            return carry

        sweep(grad, 0)
        for k, dq in enumerate(dqs):
            @pl.when(i == k)
            def _(dq=dq):
                for g in range(GROUP):
                    cols = slice(g * HD, (g + 1) * HD)
                    dq[:, cols] = (dqt[:, cols].T * INV_ROOT).astype(dq.dtype)
        return carry

    lax.fori_loop(0, len(distances), block, 0)


def first_kernel(distances, plan, lengths, *refs):
    place = here()
    n = len(distances)
    qds, refs = refs[:n], refs[n:]
    sources, refs = (refs[:NY], refs[NY:2 * NY]), refs[2 * NY:]
    dqs, refs = refs[:n], refs[n:]
    keys, values, dkeys, dvalues = refs[:4]
    z, y, c = place
    for core_rel in range(2):
        for y_rel in range(NY):
            for z_rel in range(NZ):
                chip = ((z - z_rel) & (NZ - 1)) * NY + ((y - y_rel) & (NY - 1))
                slot = chip * 2 + (c ^ core_rel)
                rows = pl.ds(pl.multiple_of(slot * BLOCK, BLOCK), BLOCK)
                keys[rows, :] = sources[core_rel][y_rel][z_rel, :, :HD]
                values[rows, :] = sources[core_rel][y_rel][z_rel, :, HD:]

    def clear(t, carry):
        rows = pl.ds(pl.multiple_of(t * TILE, TILE), TILE)
        dkeys[rows, :] = jnp.zeros((TILE, HD), jnp.float32)
        dvalues[rows, :] = jnp.zeros((TILE, HD), jnp.float32)
        return carry

    lax.fori_loop(0, SEQ // TILE, clear, 0)
    attend(place, plan, lengths, distances, qds, dqs, *refs)


def last_kernel(distances, plan, lengths, *refs):
    place = here()
    n = len(distances)
    qds, refs = refs[:n], refs[n:]
    (keys, values, dkeys_in, dvalues_in), refs = refs[:4], refs[4:]
    dqs, (keep, give, dkeys, dvalues), refs = refs[:n], refs[n:n + 4], refs[n + 4:]

    def load(t, carry):
        rows = pl.ds(pl.multiple_of(t * TILE, TILE), TILE)
        dkeys[rows, :] = dkeys_in[rows, :]
        dvalues[rows, :] = dvalues_in[rows, :]
        return carry

    lax.fori_loop(0, SEQ // TILE, load, 0)
    attend(place, plan, lengths, distances, qds, dqs, keys, values, dkeys, dvalues, *refs)
    for core_rel, chip, rows in slots(place):
        out = (keep, give)[core_rel]
        out[chip, :, :HD] = (dkeys[rows, :] * INV_ROOT).astype(out.dtype)
        out[chip, :, HD:] = dvalues[rows, :].astype(out.dtype)


def work_arrays():
    return [
        pltpu.VMEM((MAXTILES * TILE, WIDTH), jnp.float32),
        pltpu.VMEM((MAXTILES * TILE, WIDTH), jnp.float32),
        pltpu.VMEM((WIDTH, HD), jnp.bfloat16),
        pltpu.VMEM((HD, WIDTH), jnp.bfloat16),
        pltpu.VMEM((WIDTH, HD), jnp.bfloat16),
        pltpu.VMEM((HD, WIDTH), jnp.bfloat16),
        pltpu.VMEM((HD, WIDTH), jnp.float32),
    ]


def attend_first(plan, lengths, distances, qds, own, other):
    n = len(distances)
    *dqs, keys, values, dkeys, dvalues = pl.pallas_call(
        functools.partial(first_kernel, distances),
        out_shape=[jax.ShapeDtypeStruct((BLOCK, WIDTH), jnp.bfloat16)] * n
        + [jax.ShapeDtypeStruct((SEQ, HD), jnp.bfloat16)] * 2
        + [jax.ShapeDtypeStruct((SEQ, HD), jnp.float32)] * 2,
        in_specs=[SMEM] * 2 + [VMEM] * (n + 2 * NY),
        out_specs=[VMEM] * (n + 4),
        scratch_shapes=work_arrays(),
        compiler_params=pltpu.CompilerParams(vmem_limit_bytes=VMEM_BYTES),
        cost_estimate=cost(n * BLOCK_FLOPS, 8 * 2**20),
        name="attention_first",
    )(plan, lengths, *qds, *own, *other)
    return dqs, (keys, values, dkeys, dvalues)


def attend_last(plan, lengths, distances, qds, state):
    n = len(distances)
    return pl.pallas_call(
        functools.partial(last_kernel, distances),
        out_shape=[jax.ShapeDtypeStruct((BLOCK, WIDTH), jnp.bfloat16)] * n
        + [jax.ShapeDtypeStruct((NZ * NY, BLOCK, 2 * HD), jnp.bfloat16)] * 2,
        in_specs=[SMEM] * 2 + [VMEM] * (n + 4),
        out_specs=[VMEM] * (n + 2),
        scratch_shapes=[pltpu.VMEM((SEQ, HD), jnp.float32)] * 2 + work_arrays(),
        compiler_params=pltpu.CompilerParams(vmem_limit_bytes=VMEM_BYTES),
        cost_estimate=cost(n * BLOCK_FLOPS, 8 * 2**20),
        name="attention_last",
    )(plan, lengths, *qds, *state)


def shards(queries, keys, values, grad_out, lengths, plan):
    with jax.named_scope("spread_keys"):
        kv = pack(keys, values)
        row = [kv[0]] + [send(kv[d], d, 0, 0) for d in (1, 2, 3)]
        qd = pack(queries, grad_out)
        row, qd = lax.optimization_barrier((row, qd))
        row = jnp.stack(row)
        own = [row] + [send(row, 0, d, 0) for d in (1, 2, 3)]
        other = [send(part, 0, 0, 1) for part in own]
    with jax.named_scope("spread_queries"):
        near = [send(qd[d], d, 0, 0) for d in (1, 3)]
        late, near = lax.optimization_barrier((qd[2], near))
        far = send(late, 2, 0, 0)

    with jax.named_scope("attention"):
        (dq0, dq1, dq3), state = attend_first(
            plan, lengths, (0, 1, 3), (qd[0], *near), own, other
        )
        dq2, keep, give = attend_last(plan, lengths, (2,), (far,), state)

    with jax.named_scope("return_queries"):
        back1, back3 = send(dq1, -1, 0, 0), send(dq3, -3, 0, 0)
        give, back1, back3 = lax.optimization_barrier((give, back1, back3))
        grad_query = join_near(dq0, back1, back3)
        back2 = send(dq2, -2, 0, 0)

    with jax.named_scope("return_keys"):
        both = keep.astype(jnp.float32) + send(give, 0, 0, 1).astype(jnp.float32)
        both, grad_query = lax.optimization_barrier((both.astype(jnp.bfloat16), grad_query))
        partials = exchange(both)
        return tuple(finish(partials, back2, grad_query))


def solution(mesh):
    rows = P(("dp", "ctx"), None)
    return jax.shard_map(
        shards,
        mesh=mesh,
        in_specs=(rows, rows, rows, rows, P("dp"), P("dp")),
        out_specs=(rows, rows, rows),
        check_vma=False,
    )
```

profile of v0, /device:TPU:6, one launch (start us, length us, event | category | flops | bytes accessed | tf_op | source)
XLA Modules:
  0.0 96.6 jit_solution(5814417027825271243)
XLA Ops:
  0.6 0.0 copy-start
  0.6 0.0 copy-start.1
  0.7 1.6 %pack.2 = (bf16[128,256]{1,0:T(8,128)(2,1)}, bf16[128,256]{1,0:T(8,128)(2,1)}, bf16[128,256]{1,0:T(8,128)(2,1)}, bf16[128,256]{1,0:T(8,128)(2,1)}) custom-call(bf16[128,512]{1,0:T(8,128)(2,1)} %left.2, bf16[128,512]{1,0:T(8,128)(2,1)} %right.2), custom_call_target="tpu_custom_call" | custom-call | bytes 524288 | tf_op jit(solution)/shard_map/spread_keys/pack/pallas_call | solution.py:93
  2.3 0.0 copy-start.3
  2.3 2.0 %collective-permute-start = (bf16[128,256]{1,0:T(8,128)(2,1)}, bf16[128,256]{1,0:T(8,128)(2,1)S(1)}, u32[]{:S(2)}, u32[]{:S(2)}) collective-permute-start(bf16[128,256]{1,0:T(8,128)(2,1)} %get-tuple-element.38), channel_id=1, source_target_pairs={{0,8},{1,9},{2,10},{3,11},{4,12},{5,13},{6,14},{7,15},{8,16},{9,17... | collective-permute-start | bytes 196616 | tf_op jit(solution)/shard_map/spread_keys/ppermute | solution.py:63
  4.3 3.6 %collective-permute-start.1 = (bf16[128,256]{1,0:T(8,128)(2,1)}, bf16[128,256]{1,0:T(8,128)(2,1)S(1)}, u32[]{:S(2)}, u32[]{:S(2)}) collective-permute-start(bf16[128,256]{1,0:T(8,128)(2,1)} %get-tuple-element.39), channel_id=1, source_target_pairs={{0,16},{1,17},{2,18},{3,19},{4,20},{5,21},{6,22},{7,23},{8,24},{9,... | collective-permute-start | bytes 196616 | tf_op jit(solution)/shard_map/spread_keys/ppermute | solution.py:63
  7.9 1.0 %collective-permute-start.2 = (bf16[128,256]{1,0:T(8,128)(2,1)}, bf16[128,256]{1,0:T(8,128)(2,1)S(1)}, u32[]{:S(2)}, u32[]{:S(2)}) collective-permute-start(bf16[128,256]{1,0:T(8,128)(2,1)} %get-tuple-element.40), channel_id=1, source_target_pairs={{0,24},{1,25},{2,26},{3,27},{4,28},{5,29},{6,30},{7,31},{8,0},{9,1... | collective-permute-start | bytes 196616 | tf_op jit(solution)/shard_map/spread_keys/ppermute | solution.py:63
  8.9 2.9 %pack.3 = (bf16[128,2048]{1,0:T(8,128)(2,1)}, bf16[128,2048]{1,0:T(8,128)(2,1)}, bf16[128,2048]{1,0:T(8,128)(2,1)}, bf16[128,2048]{1,0:T(8,128)(2,1)}) custom-call(bf16[128,4096]{1,0:T(8,128)(2,1)} %left.3, bf16[128,4096]{1,0:T(8,128)(2,1)} %right.3), custom_call_target="tpu_custom_call" | custom-call | bytes 4194304 | tf_op jit(solution)/shard_map/spread_keys/pack/pallas_call | solution.py:93
  11.8 0.0 collective-permute-done
  11.8 0.0 collective-permute-done.1
  11.8 0.5 collective-permute-done.2
  12.4 0.6 collective-permute-start.3
  12.9 2.7 %collective-permute-start.4 = (bf16[128,2048]{1,0:T(8,128)(2,1)}, bf16[128,2048]{1,0:T(8,128)(2,1)S(1)}, u32[]{:S(2)}, u32[]{:S(2)}) collective-permute-start(bf16[128,2048]{1,0:T(8,128)(2,1)} %get-tuple-element.47), channel_id=1, source_target_pairs={{0,24},{1,25},{2,26},{3,27},{4,28},{5,29},{6,30},{7,31},{8,0},{9,1... | collective-permute-start | bytes 1572872 | tf_op jit(solution)/shard_map/spread_queries/ppermute | solution.py:63
  15.6 0.0 copy-done.3
  15.6 3.1 %collective-permute-start.8 = (bf16[4,128,256]{2,1,0:T(8,128)(2,1)S(1)}, bf16[4,128,256]{2,1,0:T(8,128)(2,1)S(1)}, u32[]{:S(2)}, u32[]{:S(2)}) collective-permute-start(bf16[4,128,256]{2,1,0:T(8,128)(2,1)S(1)} %pad_maximum_fusion.refs_3_), channel_id=1, source_target_pairs={{0,6},{1,7},{2,0},{3,1},{4,2},{5,3},{6,4},{7,5},{8,14},{9,15},{10,... | collective-permute-start | bytes 786440 | tf_op jit(solution)/shard_map/spread_keys/ppermute | solution.py:63
  18.7 0.6 collective-permute-start.7
  19.4 1.0 %collective-permute-start.6 = (bf16[4,128,256]{2,1,0:T(8,128)(2,1)S(1)}, bf16[4,128,256]{2,1,0:T(8,128)(2,1)S(1)}, u32[]{:S(2)}, u32[]{:S(2)}) collective-permute-start(bf16[4,128,256]{2,1,0:T(8,128)(2,1)S(1)} %pad_maximum_fusion.refs_3_), channel_id=1, source_target_pairs={{0,2},{1,3},{2,4},{3,5},{4,6},{5,7},{6,0},{7,1},{8,10},{9,11},{10,... | collective-permute-start | bytes 786440 | tf_op jit(solution)/shard_map/spread_keys/ppermute | solution.py:63
  20.3 7.7 %collective-permute-done.8.refs_6_ = bf16[4,128,256]{2,1,0:T(8,128)(2,1)S(1)} collective-permute-done((bf16[4,128,256]{2,1,0:T(8,128)(2,1)S(1)}, bf16[4,128,256]{2,1,0:T(8,128)(2,1)S(1)}, u32[]{:S(2)}, u32[]{:S(2)}) %collective-permute-start.8) | collective-permute-done | bytes 262176 | tf_op jit(solution)/shard_map/spread_keys/ppermute | solution.py:63
  28.1 0.0 collective-permute-start.9
  28.1 1.0 %collective-permute-done.7.refs_5_ = bf16[4,128,256]{2,1,0:T(8,128)(2,1)S(1)} collective-permute-done((bf16[4,128,256]{2,1,0:T(8,128)(2,1)S(1)}, bf16[4,128,256]{2,1,0:T(8,128)(2,1)S(1)}, u32[]{:S(2)}, u32[]{:S(2)}) %collective-permute-start.7) | collective-permute-done | bytes 262176 | tf_op jit(solution)/shard_map/spread_keys/ppermute | solution.py:63
  29.1 0.0 collective-permute-start.12
  29.1 2.7 %collective-permute-done.6.refs_4_ = bf16[4,128,256]{2,1,0:T(8,128)(2,1)S(1)} collective-permute-done((bf16[4,128,256]{2,1,0:T(8,128)(2,1)S(1)}, bf16[4,128,256]{2,1,0:T(8,128)(2,1)S(1)}, u32[]{:S(2)}, u32[]{:S(2)}) %collective-permute-start.6) | collective-permute-done | bytes 262176 | tf_op jit(solution)/shard_map/spread_keys/ppermute | solution.py:63
  31.8 0.0 collective-permute-start.11
  31.8 0.0 collective-permute-done.3.refs_1_
  31.8 0.5 collective-permute-start.10
  32.3 0.0 collective-permute-done.4.refs_2_
  32.3 0.6 collective-permute-start.5
  32.9 0.0 collective-permute-done.9.refs_7_
  32.9 0.0 collective-permute-done.12.refs_10_
  32.9 0.4 collective-permute-done.11.refs_9_
  33.3 0.4 collective-permute-done.10.refs_8_
  33.7 0.0 copy-done
  33.7 0.0 copy-done.1
  33.7 0.0 copy-start.2
  33.7 1.0 %copy-done.2 = bf16[128,2048]{1,0:T(8,128)(2,1)S(1)} copy-done((bf16[128,2048]{1,0:T(8,128)(2,1)S(1)}, bf16[128,2048]{1,0:T(8,128)(2,1)}, u32[]{:S(2)}) %copy-start.2) | copy-done | bytes 524312
  34.7 14.4 %attention_first.1 = (bf16[128,1024]{1,0:T(8,128)(2,1)S(1)}, bf16[128,1024]{1,0:T(8,128)(2,1)S(1)}, bf16[128,1024]{1,0:T(8,128)(2,1)S(1)}, bf16[4096,128]{1,0:T(...) custom-call(s32[32]{0:T(128)S(1)} %copy-done, s32[8]{0:T(128)S(1)} %copy-done.1, ...), custom_call_target="tpu_custom_call" | custom-call | flops 4026531840 | bytes 8388608 | tf_op jit(solution)/shard_map/attention/attention_first/pallas_call | solution.py:376
  49.2 0.1 collective-permute-start.13
  49.3 2.0 %collective-permute-start.14 = (bf16[128,1024]{1,0:T(8,128)(2,1)S(1)}, bf16[128,1024]{1,0:T(8,128)(2,1)S(1)}, u32[]{:S(2)}, u32[]{:S(2)}) collective-permute-start(bf16[128,1024]{1,0:T(8,128)(2,1)S(1)} %get-tuple-element.63), channel_id=1, source_target_pairs={{0,8},{1,9},{2,10},{3,11},{4,12},{5,13},{6,14},{7,15},{8,16},{9,17... | collective-permute-start | bytes 786440 | tf_op jit(solution)/shard_map/return_queries/ppermute | solution.py:63
  51.3 0.0 collective-permute-done.5.refs_0_
  51.3 2.9 %attention_last.1 = (bf16[128,1024]{1,0:T(8,128)(2,1)S(1)}, bf16[16,128,256]{2,1,0:T(8,128)(2,1)S(1)}, bf16[16,128,256]{2,1,0:T(8,128)(2,1)S(1)}) custom-call(s32[32]{0:T(128)S(1)} %copy-done, s32[8]{0:T(128)S(1)} %copy-done.1, bf16[128,2048]{1,0:T(8,128)(2,1)S(1)} %collective-permute-done.5.refs_0_, bf16[4096,128]{1,0:T(8,128)(2,1)S(1)} %get-tuple-element.56.refs_1_, ...), custom_call_target="tpu_custom_call" | custom-call | flops 1342177280 | bytes 8388608 | tf_op jit(solution)/shard_map/attention/attention_last/pallas_call | solution.py:393
  54.2 1.6 %collective-permute-done.13.dq1 = bf16[128,1024]{1,0:T(8,128)(2,1)S(1)} collective-permute-done((bf16[128,1024]{1,0:T(8,128)(2,1)S(1)}, bf16[128,1024]{1,0:T(8,128)(2,1)S(1)}, u32[]{:S(2)}, u32[]{:S(2)}) %collective-permute-start.13) | collective-permute-done | bytes 262176 | tf_op jit(solution)/shard_map/return_queries/ppermute | solution.py:63
  55.8 2.6 %collective-permute-done.14.dq3 = bf16[128,1024]{1,0:T(8,128)(2,1)S(1)} collective-permute-done((bf16[128,1024]{1,0:T(8,128)(2,1)S(1)}, bf16[128,1024]{1,0:T(8,128)(2,1)S(1)}, u32[]{:S(2)}, u32[]{:S(2)}) %collective-permute-start.14) | collective-permute-done | bytes 262176 | tf_op jit(solution)/shard_map/return_queries/ppermute | solution.py:63
  58.3 0.0 collective-permute-start.15
  58.3 1.2 %join_near.1.grad_in = f32[128,4096]{1,0:T(8,128)} custom-call(bf16[128,1024]{1,0:T(8,128)(2,1)S(1)} %get-tuple-element.65.dq0, bf16[128,1024]{1,0:T(8,128)(2,1)S(1)} %collective-permute-done.13.dq1, bf16[128,1024]{1,0:T(8,128)(2,1)S(1)} %collective-permute-done.14.dq3), custom_call_target="tpu_custom_call" | custom-call | bytes 3145728 | tf_op jit(solution)/shard_map/return_queries/join_near/pallas_call | solution.py:122
  59.5 1.5 %collective-permute-done.15 = bf16[16,128,256]{2,1,0:T(8,128)(2,1)S(1)} collective-permute-done((bf16[16,128,256]{2,1,0:T(8,128)(2,1)S(1)}, bf16[16,128,256]{2,1,0:T(8,128)(2,1)S(1)}, u32[]{:S(2)}, u32[]{:S(2)}) %collective-permute-start.15) | collective-permute-done | bytes 1048608 | tf_op jit(solution)/shard_map/return_keys/ppermute | solution.py:63
  61.0 1.4 %add_convert_fusion = bf16[16,128,256]{2,1,0:T(8,128)(2,1)} fusion(bf16[16,128,256]{2,1,0:T(8,128)(2,1)S(1)} %collective-permute-done.15, bf16[16,128,256]{2,1,0:T(8,128)(2,1)S(1)} %get-tuple-element.60), kind=kLoop, calls=%fused_computation | loop fusion | flops 2097152 | bytes 3145728 | tf_op jit(solution)/shard_map/return_keys/convert_element_type | solution.py:434
  62.4 11.5 %all-to-all-start = ((bf16[16,128,256]{2,1,0:T(8,128)(2,1)}), bf16[16,128,256]{2,1,0:T(8,128)(2,1)S(1)}, u32[]{:S(2)}, u32[]{:S(2)}) async-start(bf16[16,128,256]{2,1,0:T(8,128)(2,1)} %add_convert_fusion), calls=%async_computation | async-start | bytes 2097152 | tf_op jit(solution)/shard_map/return_keys/all_to_all | solution.py:57
  73.9 3.4 %collective-permute-start.16 = (bf16[128,1024]{1,0:T(8,128)(2,1)S(1)}, bf16[128,1024]{1,0:T(8,128)(2,1)S(1)}, u32[]{:S(2)}, u32[]{:S(2)}) collective-permute-start(bf16[128,1024]{1,0:T(8,128)(2,1)S(1)} %get-tuple-element.69), channel_id=1, source_target_pairs={{0,16},{1,17},{2,18},{3,19},{4,20},{5,21},{6,22},{7,23},{8,24},{9,... | collective-permute-start | bytes 786440 | tf_op jit(solution)/shard_map/return_queries/ppermute | solution.py:63
  77.3 17.5 %collective-permute-done.16.dq2 = bf16[128,1024]{1,0:T(8,128)(2,1)S(1)} collective-permute-done((bf16[128,1024]{1,0:T(8,128)(2,1)S(1)}, bf16[128,1024]{1,0:T(8,128)(2,1)S(1)}, u32[]{:S(2)}, u32[]{:S(2)}) %collective-permute-start.16) | collective-permute-done | bytes 262176 | tf_op jit(solution)/shard_map/return_queries/ppermute | solution.py:63
  94.8 0.0 all-to-all-done.partials
  94.8 1.6 %finish.1 = (f32[128,4096]{1,0:T(8,128)}, f32[128,512]{1,0:T(8,128)}, f32[128,512]{1,0:T(8,128)}) custom-call(bf16[16,128,256]{2,1,0:T(8,128)(2,1)S(1)} %all-to-all-done.partials, bf16[128,1024]{1,0:T(8,128)(2,1)S(1)} %collective-permute-done.16.dq2, f32[128,4096]{1,0:T(8,128)} %join_near.1.grad_in), custom_call_target="tpu_custom_call", output_to_operand_aliasing={{0}: (2, {})} | custom-call | bytes 4194304 | tf_op jit(solution)/shard_map/return_keys/finish/pallas_call | solution.py:150
  (1 shorter events, 0.0 us)
Async XLA Ops:
  0.6 33.1 %copy-start = (s32[32]{0:T(128)S(1)}, s32[32]{0:T(128)}, u32[]{:S(2)}) copy-start(s32[32]{0:T(128)} %plan.3) | copy-start | bytes 388
  0.6 33.0 %copy-start.1 = (s32[8]{0:T(128)S(1)}, s32[8]{0:T(128)}, u32[]{:S(2)}) copy-start(s32[8]{0:T(128)} %lengths.3) | copy-start | bytes 100
  2.3 13.3 %copy-start.3 = (bf16[128,256]{1,0:T(8,128)(2,1)S(1)}, bf16[128,256]{1,0:T(8,128)(2,1)}, u32[]{:S(2)}) copy-start(bf16[128,256]{1,0:T(8,128)(2,1)} %get-tuple-element.52) | copy-start | bytes 196612
  2.3 9.5 %collective-permute-start = (bf16[128,256]{1,0:T(8,128)(2,1)}, bf16[128,256]{1,0:T(8,128)(2,1)S(1)}, u32[]{:S(2)}, u32[]{:S(2)}) collective-permute-start(bf16[128,256]{1,0:T(8,128)(2,1)} %get-tuple-element.38), channel_id=1, source_target_pairs={{0,8},{1,9},{2,10},{3,11},{4,12},{5,13},{6,14},{7,15},{8,16},{9,17... | collective-permute-start | bytes 196616 | tf_op jit(solution)/shard_map/spread_keys/ppermute | solution.py:63
  4.3 7.5 %collective-permute-start.1 = (bf16[128,256]{1,0:T(8,128)(2,1)}, bf16[128,256]{1,0:T(8,128)(2,1)S(1)}, u32[]{:S(2)}, u32[]{:S(2)}) collective-permute-start(bf16[128,256]{1,0:T(8,128)(2,1)} %get-tuple-element.39), channel_id=1, source_target_pairs={{0,16},{1,17},{2,18},{3,19},{4,20},{5,21},{6,22},{7,23},{8,24},{9,... | collective-permute-start | bytes 196616 | tf_op jit(solution)/shard_map/spread_keys/ppermute | solution.py:63
  7.9 4.5 %collective-permute-start.2 = (bf16[128,256]{1,0:T(8,128)(2,1)}, bf16[128,256]{1,0:T(8,128)(2,1)S(1)}, u32[]{:S(2)}, u32[]{:S(2)}) collective-permute-start(bf16[128,256]{1,0:T(8,128)(2,1)} %get-tuple-element.40), channel_id=1, source_target_pairs={{0,24},{1,25},{2,26},{3,27},{4,28},{5,29},{6,30},{7,31},{8,0},{9,1... | collective-permute-start | bytes 196616 | tf_op jit(solution)/shard_map/spread_keys/ppermute | solution.py:63
  12.4 19.4 %collective-permute-start.3 = (bf16[128,2048]{1,0:T(8,128)(2,1)}, bf16[128,2048]{1,0:T(8,128)(2,1)S(1)}, u32[]{:S(2)}, u32[]{:S(2)}) collective-permute-start(bf16[128,2048]{1,0:T(8,128)(2,1)} %get-tuple-element.46), channel_id=1, source_target_pairs={{0,8},{1,9},{2,10},{3,11},{4,12},{5,13},{6,14},{7,15},{8,16},{9,17... | collective-permute-start | bytes 1572872 | tf_op jit(solution)/shard_map/spread_queries/ppermute | solution.py:63
  12.9 19.4 %collective-permute-start.4 = (bf16[128,2048]{1,0:T(8,128)(2,1)}, bf16[128,2048]{1,0:T(8,128)(2,1)S(1)}, u32[]{:S(2)}, u32[]{:S(2)}) collective-permute-start(bf16[128,2048]{1,0:T(8,128)(2,1)} %get-tuple-element.47), channel_id=1, source_target_pairs={{0,24},{1,25},{2,26},{3,27},{4,28},{5,29},{6,30},{7,31},{8,0},{9,1... | collective-permute-start | bytes 1572872 | tf_op jit(solution)/shard_map/spread_queries/ppermute | solution.py:63
  15.6 12.4 %collective-permute-start.8 = (bf16[4,128,256]{2,1,0:T(8,128)(2,1)S(1)}, bf16[4,128,256]{2,1,0:T(8,128)(2,1)S(1)}, u32[]{:S(2)}, u32[]{:S(2)}) collective-permute-start(bf16[4,128,256]{2,1,0:T(8,128)(2,1)S(1)} %pad_maximum_fusion.refs_3_), channel_id=1, source_target_pairs={{0,6},{1,7},{2,0},{3,1},{4,2},{5,3},{6,4},{7,5},{8,14},{9,15},{10,... | collective-permute-start | bytes 786440 | tf_op jit(solution)/shard_map/spread_keys/ppermute | solution.py:63
  18.7 10.3 %collective-permute-start.7 = (bf16[4,128,256]{2,1,0:T(8,128)(2,1)S(1)}, bf16[4,128,256]{2,1,0:T(8,128)(2,1)S(1)}, u32[]{:S(2)}, u32[]{:S(2)}) collective-permute-start(bf16[4,128,256]{2,1,0:T(8,128)(2,1)S(1)} %pad_maximum_fusion.refs_3_), channel_id=1, source_target_pairs={{0,4},{1,5},{2,6},{3,7},{4,0},{5,1},{6,2},{7,3},{8,12},{9,13},{10,... | collective-permute-start | bytes 786440 | tf_op jit(solution)/shard_map/spread_keys/ppermute | solution.py:63
  19.4 12.4 %collective-permute-start.6 = (bf16[4,128,256]{2,1,0:T(8,128)(2,1)S(1)}, bf16[4,128,256]{2,1,0:T(8,128)(2,1)S(1)}, u32[]{:S(2)}, u32[]{:S(2)}) collective-permute-start(bf16[4,128,256]{2,1,0:T(8,128)(2,1)S(1)} %pad_maximum_fusion.refs_3_), channel_id=1, source_target_pairs={{0,2},{1,3},{2,4},{3,5},{4,6},{5,7},{6,0},{7,1},{8,10},{9,11},{10,... | collective-permute-start | bytes 786440 | tf_op jit(solution)/shard_map/spread_keys/ppermute | solution.py:63
  28.1 4.8 %collective-permute-start.9 = (bf16[4,128,256]{2,1,0:T(8,128)(2,1)S(1)}, bf16[4,128,256]{2,1,0:T(8,128)(2,1)S(1)}, u32[]{:S(2)}, u32[]{:S(2)}) collective-permute-start(bf16[4,128,256]{2,1,0:T(8,128)(2,1)S(1)} %pad_maximum_fusion.refs_3_), channel_id=1, source_target_pairs={{0,1},{1,0},{2,3},{3,2},{4,5},{5,4},{6,7},{7,6},{8,9},{9,8},{10,11... | collective-permute-start | bytes 786440 | tf_op jit(solution)/shard_map/spread_keys/ppermute | solution.py:63
  29.1 3.9 %collective-permute-start.12 = (bf16[4,128,256]{2,1,0:T(8,128)(2,1)S(1)}, bf16[4,128,256]{2,1,0:T(8,128)(2,1)S(1)}, u32[]{:S(2)}, u32[]{:S(2)}) collective-permute-start(bf16[4,128,256]{2,1,0:T(8,128)(2,1)S(1)} %collective-permute-done.8.refs_6_), channel_id=1, source_target_pairs={{0,1},{1,0},{2,3},{3,2},{4,5},{5,4},{6,7},{7,6},{8,9},{9,8},{10,11... | collective-permute-start | bytes 786440 | tf_op jit(solution)/shard_map/spread_keys/ppermute | solution.py:63
  31.8 1.5 %collective-permute-start.11 = (bf16[4,128,256]{2,1,0:T(8,128)(2,1)S(1)}, bf16[4,128,256]{2,1,0:T(8,128)(2,1)S(1)}, u32[]{:S(2)}, u32[]{:S(2)}) collective-permute-start(bf16[4,128,256]{2,1,0:T(8,128)(2,1)S(1)} %collective-permute-done.7.refs_5_), channel_id=1, source_target_pairs={{0,1},{1,0},{2,3},{3,2},{4,5},{5,4},{6,7},{7,6},{8,9},{9,8},{10,11... | collective-permute-start | bytes 786440 | tf_op jit(solution)/shard_map/spread_keys/ppermute | solution.py:63
  31.8 1.9 %collective-permute-start.10 = (bf16[4,128,256]{2,1,0:T(8,128)(2,1)S(1)}, bf16[4,128,256]{2,1,0:T(8,128)(2,1)S(1)}, u32[]{:S(2)}, u32[]{:S(2)}) collective-permute-start(bf16[4,128,256]{2,1,0:T(8,128)(2,1)S(1)} %collective-permute-done.6.refs_4_), channel_id=1, source_target_pairs={{0,1},{1,0},{2,3},{3,2},{4,5},{5,4},{6,7},{7,6},{8,9},{9,8},{10,11... | collective-permute-start | bytes 786440 | tf_op jit(solution)/shard_map/spread_keys/ppermute | solution.py:63
  32.3 19.0 %collective-permute-start.5 = (bf16[128,2048]{1,0:T(8,128)(2,1)}, bf16[128,2048]{1,0:T(8,128)(2,1)S(1)}, u32[]{:S(2)}, u32[]{:S(2)}) collective-permute-start(bf16[128,2048]{1,0:T(8,128)(2,1)} %get-tuple-element.48), channel_id=1, source_target_pairs={{0,16},{1,17},{2,18},{3,19},{4,20},{5,21},{6,22},{7,23},{8,24},{9,... | collective-permute-start | bytes 1572872 | tf_op jit(solution)/shard_map/spread_queries/ppermute | solution.py:63
  33.7 1.0 %copy-start.2 = (bf16[128,2048]{1,0:T(8,128)(2,1)S(1)}, bf16[128,2048]{1,0:T(8,128)(2,1)}, u32[]{:S(2)}) copy-start(bf16[128,2048]{1,0:T(8,128)(2,1)} %get-tuple-element.49.refs_0_) | copy-start | bytes 1572868
  49.2 6.6 %collective-permute-start.13 = (bf16[128,1024]{1,0:T(8,128)(2,1)S(1)}, bf16[128,1024]{1,0:T(8,128)(2,1)S(1)}, u32[]{:S(2)}, u32[]{:S(2)}) collective-permute-start(bf16[128,1024]{1,0:T(8,128)(2,1)S(1)} %get-tuple-element.62), channel_id=1, source_target_pairs={{0,24},{1,25},{2,26},{3,27},{4,28},{5,29},{6,30},{7,31},{8,0},{9,1... | collective-permute-start | bytes 786440 | tf_op jit(solution)/shard_map/return_queries/ppermute | solution.py:63
  49.3 9.1 %collective-permute-start.14 = (bf16[128,1024]{1,0:T(8,128)(2,1)S(1)}, bf16[128,1024]{1,0:T(8,128)(2,1)S(1)}, u32[]{:S(2)}, u32[]{:S(2)}) collective-permute-start(bf16[128,1024]{1,0:T(8,128)(2,1)S(1)} %get-tuple-element.63), channel_id=1, source_target_pairs={{0,8},{1,9},{2,10},{3,11},{4,12},{5,13},{6,14},{7,15},{8,16},{9,17... | collective-permute-start | bytes 786440 | tf_op jit(solution)/shard_map/return_queries/ppermute | solution.py:63
  58.3 2.7 %collective-permute-start.15 = (bf16[16,128,256]{2,1,0:T(8,128)(2,1)S(1)}, bf16[16,128,256]{2,1,0:T(8,128)(2,1)S(1)}, u32[]{:S(2)}, u32[]{:S(2)}) collective-permute-start(bf16[16,128,256]{2,1,0:T(8,128)(2,1)S(1)} %get-tuple-element.64), channel_id=1, source_target_pairs={{0,1},{1,0},{2,3},{3,2},{4,5},{5,4},{6,7},{7,6},{8,9},{9,8},{10,11... | collective-permute-start | bytes 3145736 | tf_op jit(solution)/shard_map/return_keys/ppermute | solution.py:63
  62.4 32.4 %all-to-all-start = ((bf16[16,128,256]{2,1,0:T(8,128)(2,1)}), bf16[16,128,256]{2,1,0:T(8,128)(2,1)S(1)}, u32[]{:S(2)}, u32[]{:S(2)}) async-start(bf16[16,128,256]{2,1,0:T(8,128)(2,1)} %add_convert_fusion), calls=%async_computation | async-start | bytes 2097152 | tf_op jit(solution)/shard_map/return_keys/all_to_all | solution.py:57
  73.9 20.9 %collective-permute-start.16 = (bf16[128,1024]{1,0:T(8,128)(2,1)S(1)}, bf16[128,1024]{1,0:T(8,128)(2,1)S(1)}, u32[]{:S(2)}, u32[]{:S(2)}) collective-permute-start(bf16[128,1024]{1,0:T(8,128)(2,1)S(1)} %get-tuple-element.69), channel_id=1, source_target_pairs={{0,16},{1,17},{2,18},{3,19},{4,20},{5,21},{6,22},{7,23},{8,24},{9,... | collective-permute-start | bytes 786440 | tf_op jit(solution)/shard_map/return_queries/ppermute | solution.py:63
where the time goes:
time: 97 us; the launch traced here: 96.6 us
  waiting for transfers between devices  35.8 us (37%)
  starting transfers between devices  32.7 us (34%)
  Pallas kernels  24.8 us (26%)
  other arithmetic  1.4 us (1%)
  local copies, waits for them, and re-layouts  1.06 us (1%)
    ppermute x17, waiting for transfers between devices, send(): return lax.ppermute(x, 'ctx', ring(dz, dy, dc))  35.8 us
    ppermute x17, starting transfers between devices, send(): return lax.ppermute(x, 'ctx', ring(dz, dy, dc))  21.2 us
    pallas_call x1, Pallas kernels, attend_first(): pl.pallas_call(functools.partial(first_kernel, distances), out_shape=[jax...  14.4 us
    all_to_all x1, starting transfers between devices, exchange(): lax.all_to_all(x, 'ctx', split_axis=0, concat_axis=0, axis_index_groups=S...  11.5 us
    pallas_call x2, Pallas kernels, pack(): pl.pallas_call(functools.partial(pack_kernel, width), out_shape=[jax.Shap...  4.56 us
    pallas_call x1, Pallas kernels, attend_last(): pl.pallas_call(functools.partial(last_kernel, distances), out_shape=[jax....  2.94 us
  transfers between devices with their start and end apart: 18, of which 10 were waited for; matrix products, arithmetic and copies ran while one was open for 0% of the time, Pallas kernels for 22%

commit v1 on v0

--- a/solution.py
+++ b/solution.py
@@ -50,15 +50,6 @@
     ]
 
 
-SAME_CORE = [[chip * 2 + core for chip in range(NZ * NY)] for core in range(2)]
-
-
-def exchange(x):
-    return lax.all_to_all(
-        x, "ctx", split_axis=0, concat_axis=0, axis_index_groups=SAME_CORE, tiled=True
-    )
-
-
 def send(x, dz, dy, dc):
     return lax.ppermute(x, "ctx", ring(dz, dy, dc))
 
@@ -88,7 +79,7 @@
         copy.wait()
 
 
-def pack(left, right):
+def pack(left, right, vmem_bytes):
     width = left.shape[1] // KVH
     return pl.pallas_call(
         functools.partial(pack_kernel, width),
@@ -96,7 +87,7 @@
         in_specs=[HBM] * 2,
         out_specs=[VMEM] * NZ,
         scratch_shapes=[pltpu.SemaphoreType.DMA((2 * NZ,))],
-        compiler_params=pltpu.CompilerParams(vmem_limit_bytes=PACK_VMEM_BYTES),
+        compiler_params=pltpu.CompilerParams(vmem_limit_bytes=vmem_bytes),
         cost_estimate=cost(0, 4 * left.size * 2),
         name="pack",
     )(left, right)
@@ -113,14 +104,14 @@
     return copies
 
 
-def join_near_kernel(dq0, dq1, dq3, out, wide, sems):
-    for copy in put_heads(here(), ((0, dq0), (1, dq1), (3, dq3)), out, wide, sems):
+def join_early_kernel(dq0, dq1, dq2, out, wide, sems):
+    for copy in put_heads(here(), ((0, dq0), (1, dq1), (2, dq2)), out, wide, sems):
         copy.wait()
 
 
-def join_near(dq0, dq1, dq3):
+def join_early(dq0, dq1, dq2):
     return pl.pallas_call(
-        join_near_kernel,
+        join_early_kernel,
         out_shape=jax.ShapeDtypeStruct((BLOCK, KVH * WIDTH), jnp.float32),
         in_specs=[VMEM] * 3,
         out_specs=HBM,
@@ -130,30 +121,28 @@
         ],
         compiler_params=pltpu.CompilerParams(vmem_limit_bytes=SMALL_VMEM_BYTES),
         cost_estimate=cost(0, BLOCK * KVH * WIDTH * 6),
-        name="join_near",
-    )(dq0, dq1, dq3)
-
-
-def finish_kernel(partials, dq2, grad_in, out, dk, dv, wide, sems):
-    copies = put_heads(here(), ((2, dq2),), out, wide, sems)
-    for h in range(KVH):
-        total = partials[h * NY].astype(jnp.float32)
-        for y in range(1, NY):
-            total = total + partials[h * NY + y].astype(jnp.float32)
-        dk[:, h * HD:(h + 1) * HD] = total[:, :HD]
-        dv[:, h * HD:(h + 1) * HD] = total[:, HD:]
+        name="join_early",
+    )(dq0, dq1, dq2)
+
+
+def finish_kernel(part0, part1, part2, part3, dq3, grad_in, out, dk, dv, wide, sems):
+    place = here()
+    copies = put_heads(place, ((3, dq3),), out, wide, sems)
+    for d, part in enumerate((part0, part1, part2, part3)):
+        dk[:, at_head(place, -d, HD)] = part[:, :HD].astype(dk.dtype)
+        dv[:, at_head(place, -d, HD)] = part[:, HD:].astype(dv.dtype)
     for copy in copies:
         copy.wait()
 
 
-def finish(partials, dq2, grad_query):
+def finish(parts, dq3, grad_query):
     return pl.pallas_call(
         finish_kernel,
         out_shape=[jax.ShapeDtypeStruct((BLOCK, KVH * WIDTH), jnp.float32)]
         + [jax.ShapeDtypeStruct((BLOCK, KVH * HD), jnp.float32)] * 2,
-        in_specs=[VMEM, VMEM, HBM],
+        in_specs=[VMEM] * (NZ + 1) + [HBM],
         out_specs=[HBM, VMEM, VMEM],
-        input_output_aliases={2: 0},
+        input_output_aliases={NZ + 1: 0},
         scratch_shapes=[
             pltpu.VMEM((1, BLOCK, WIDTH), jnp.float32),
             pltpu.SemaphoreType.DMA((1,)),
@@ -161,14 +150,17 @@
         compiler_params=pltpu.CompilerParams(vmem_limit_bytes=SMALL_VMEM_BYTES),
         cost_estimate=cost(0, 4 * 2**20),
         name="finish",
-    )(partials, dq2, grad_query)
-
-
-def slots(place):
+    )(*parts, dq3, grad_query)
+
+
+def slots(place, sign):
+    z, y, c = place
     for core_rel in range(2):
-        for chip in range(NZ * NY):
-            slot = chip * 2 + (place[2] ^ core_rel)
-            yield core_rel, chip, pl.ds(pl.multiple_of(slot * BLOCK, BLOCK), BLOCK)
+        for y_rel in range(NY):
+            for z_rel in range(NZ):
+                chip = ((z + sign * z_rel) & (NZ - 1)) * NY + ((y + sign * y_rel) & (NY - 1))
+                slot = chip * 2 + (c ^ core_rel)
+                yield core_rel, y_rel, z_rel, pl.ds(pl.multiple_of(slot * BLOCK, BLOCK), BLOCK)
 
 
 def attend(
@@ -318,15 +310,9 @@
     sources, refs = (refs[:NY], refs[NY:2 * NY]), refs[2 * NY:]
     dqs, refs = refs[:n], refs[n:]
     keys, values, dkeys, dvalues = refs[:4]
-    z, y, c = place
-    for core_rel in range(2):
-        for y_rel in range(NY):
-            for z_rel in range(NZ):
-                chip = ((z - z_rel) & (NZ - 1)) * NY + ((y - y_rel) & (NY - 1))
-                slot = chip * 2 + (c ^ core_rel)
-                rows = pl.ds(pl.multiple_of(slot * BLOCK, BLOCK), BLOCK)
-                keys[rows, :] = sources[core_rel][y_rel][z_rel, :, :HD]
-                values[rows, :] = sources[core_rel][y_rel][z_rel, :, HD:]
+    for core_rel, y_rel, z_rel, rows in slots(place, -1):
+        keys[rows, :] = sources[core_rel][y_rel][z_rel, :, :HD]
+        values[rows, :] = sources[core_rel][y_rel][z_rel, :, HD:]
 
     def clear(t, carry):
         rows = pl.ds(pl.multiple_of(t * TILE, TILE), TILE)
@@ -353,10 +339,10 @@
 
     lax.fori_loop(0, SEQ // TILE, load, 0)
     attend(place, plan, lengths, distances, qds, dqs, keys, values, dkeys, dvalues, *refs)
-    for core_rel, chip, rows in slots(place):
+    for core_rel, y_rel, z_rel, rows in slots(place, 1):
         out = (keep, give)[core_rel]
-        out[chip, :, :HD] = (dkeys[rows, :] * INV_ROOT).astype(out.dtype)
-        out[chip, :, HD:] = dvalues[rows, :].astype(out.dtype)
+        out[y_rel, z_rel, :, :HD] = (dkeys[rows, :] * INV_ROOT).astype(out.dtype)
+        out[y_rel, z_rel, :, HD:] = dvalues[rows, :].astype(out.dtype)
 
 
 def work_arrays():
@@ -393,7 +379,7 @@
     return pl.pallas_call(
         functools.partial(last_kernel, distances),
         out_shape=[jax.ShapeDtypeStruct((BLOCK, WIDTH), jnp.bfloat16)] * n
-        + [jax.ShapeDtypeStruct((NZ * NY, BLOCK, 2 * HD), jnp.bfloat16)] * 2,
+        + [jax.ShapeDtypeStruct((NY, NZ, BLOCK, 2 * HD), jnp.bfloat16)] * 2,
         in_specs=[SMEM] * 2 + [VMEM] * (n + 4),
         out_specs=[VMEM] * (n + 2),
         scratch_shapes=[pltpu.VMEM((SEQ, HD), jnp.float32)] * 2 + work_arrays(),
@@ -405,9 +391,9 @@
 
 def shards(queries, keys, values, grad_out, lengths, plan):
     with jax.named_scope("spread_keys"):
-        kv = pack(keys, values)
+        kv = pack(keys, values, PACK_VMEM_BYTES)
         row = [kv[0]] + [send(kv[d], d, 0, 0) for d in (1, 2, 3)]
-        qd = pack(queries, grad_out)
+        qd = pack(queries, grad_out, SMALL_VMEM_BYTES)
         row, qd = lax.optimization_barrier((row, qd))
         row = jnp.stack(row)
         own = [row] + [send(row, 0, d, 0) for d in (1, 2, 3)]
@@ -423,17 +409,20 @@
         )
         dq2, keep, give = attend_last(plan, lengths, (2,), (far,), state)
 
-    with jax.named_scope("return_queries"):
-        back1, back3 = send(dq1, -1, 0, 0), send(dq3, -3, 0, 0)
-        give, back1, back3 = lax.optimization_barrier((give, back1, back3))
-        grad_query = join_near(dq0, back1, back3)
-        back2 = send(dq2, -2, 0, 0)
-
     with jax.named_scope("return_keys"):
         both = keep.astype(jnp.float32) + send(give, 0, 0, 1).astype(jnp.float32)
-        both, grad_query = lax.optimization_barrier((both.astype(jnp.bfloat16), grad_query))
-        partials = exchange(both)
-        return tuple(finish(partials, back2, grad_query))
+        both = both.astype(jnp.bfloat16)
+        back1, back2 = send(dq1, -1, 0, 0), send(dq2, -2, 0, 0)
+        grad_query = join_early(dq0, back1, back2)
+        parts = [send(both[d], 0, d, 0) for d in (1, 2, 3)]
+        parts, dq3, grad_query = lax.optimization_barrier((parts, dq3, grad_query))
+        back3 = send(dq3, -3, 0, 0)
+        total = both[0].astype(jnp.float32)
+        for part in parts:
+            total = total + part.astype(jnp.float32)
+        total = total.astype(jnp.bfloat16)
+        heads = [total[0]] + [send(total[d], d, 0, 0) for d in (1, 2, 3)]
+        return tuple(finish(heads, back3, grad_query))
 
 
 def solution(mesh):

time: 97 us -> 92.1 us (0.949)
  Pallas kernels: 24.8 us -> 21 us
  waiting for transfers between devices: 35.8 us -> 33.5 us
  local copies, waits for them, and re-layouts: 1.06 us -> 2.53 us
    ppermute x17 -> x23, starting transfers between devices: 21.2 us -> 33.4 us  [send(): return lax.ppermute(x, 'ctx', ring(dz, dy, dc))]
    all_to_all x1 -> x0, starting transfers between devices: 11.5 us -> none  [exchange(): lax.all_to_all(x, 'ctx', split_axis=0, concat_axis=0, axis_index_groups=S...]
    pallas_call x2, Pallas kernels: 4.56 us -> 1.89 us  [pack(): pl.pallas_call(functools.partial(pack_kernel, width), out_shape=[jax.Shap...]
    ppermute x17 -> x23, waiting for transfers between devices: 35.8 us -> 33.5 us  [send(): return lax.ppermute(x, 'ctx', ring(dz, dy, dc))]
    unnamed x8 -> x10, local copies, waits for them, and re-layouts: 1.06 us -> 2.46 us
    pallas_call x1, Pallas kernels: 14.4 us -> 13.4 us  [attend_first(): pl.pallas_call(functools.partial(first_kernel, distances), out_shape=[jax...]
  transfers between devices with their start and end apart: 18 -> 23, of which waited for: 10 -> 15; matrix products, arithmetic and copies ran while one was open for 0% -> 1% of each run, Pallas kernels for 22% -> 16%
where the time goes in v1:
time: 92.1 us; the launch traced here: 92 us
  waiting for transfers between devices  33.5 us (36%)
  starting transfers between devices  33.4 us (36%)
  Pallas kernels  21 us (23%)
  local copies, waits for them, and re-layouts  2.53 us (3%)
  between operations  0.93 us (1%)
    ppermute x23, waiting for transfers between devices, send(): return lax.ppermute(x, 'ctx', ring(dz, dy, dc))  33.5 us
    ppermute x23, starting transfers between devices, send(): return lax.ppermute(x, 'ctx', ring(dz, dy, dc))  33.4 us
    pallas_call x1, Pallas kernels, attend_first(): pl.pallas_call(functools.partial(first_kernel, distances), out_shape=[jax...  13.4 us
    pallas_call x1, Pallas kernels, attend_last(): pl.pallas_call(functools.partial(last_kernel, distances), out_shape=[jax....  2.94 us
    unnamed x10, local copies, waits for them, and re-layouts  2.46 us
    pallas_call x2, Pallas kernels, pack(): pl.pallas_call(functools.partial(pack_kernel, width), out_shape=[jax.Shap...  1.89 us
  transfers between devices with their start and end apart: 23, of which 15 were waited for; matrix products, arithmetic and copies ran while one was open for 1% of the time, Pallas kernels for 16%

profile of v1, /device:TPU:6, one launch (start us, length us, event | category | flops | bytes accessed | tf_op | source)
XLA Modules:
  0.0 92.0 jit_solution(1073685159493557598)
XLA Ops:
  0.6 0.0 copy-start.2
  0.6 0.0 copy-start.3
  0.7 1.6 %pack.2 = (bf16[128,256]{1,0:T(8,128)(2,1)}, bf16[128,256]{1,0:T(8,128)(2,1)}, bf16[128,256]{1,0:T(8,128)(2,1)}, bf16[128,256]{1,0:T(8,128)(2,1)}) custom-call(bf16[128,512]{1,0:T(8,128)(2,1)} %left.2, bf16[128,512]{1,0:T(8,128)(2,1)} %right.2), custom_call_target="tpu_custom_call" | custom-call | bytes 524288 | tf_op jit(solution)/shard_map/spread_keys/pack/pallas_call | solution.py:84
  2.3 2.0 %collective-permute-start = (bf16[128,256]{1,0:T(8,128)(2,1)}, bf16[128,256]{1,0:T(8,128)(2,1)S(1)}, u32[]{:S(2)}, u32[]{:S(2)}) collective-permute-start(bf16[128,256]{1,0:T(8,128)(2,1)} %get-tuple-element.38), channel_id=1, source_target_pairs={{0,8},{1,9},{2,10},{3,11},{4,12},{5,13},{6,14},{7,15},{8,16},{9,17... | collective-permute-start | bytes 196616 | tf_op jit(solution)/shard_map/spread_keys/ppermute | solution.py:54
  4.3 3.6 %collective-permute-start.1 = (bf16[128,256]{1,0:T(8,128)(2,1)}, bf16[128,256]{1,0:T(8,128)(2,1)S(1)}, u32[]{:S(2)}, u32[]{:S(2)}) collective-permute-start(bf16[128,256]{1,0:T(8,128)(2,1)} %get-tuple-element.39), channel_id=1, source_target_pairs={{0,16},{1,17},{2,18},{3,19},{4,20},{5,21},{6,22},{7,23},{8,24},{9,... | collective-permute-start | bytes 196616 | tf_op jit(solution)/shard_map/spread_keys/ppermute | solution.py:54
  7.9 1.0 %collective-permute-start.2 = (bf16[128,256]{1,0:T(8,128)(2,1)}, bf16[128,256]{1,0:T(8,128)(2,1)S(1)}, u32[]{:S(2)}, u32[]{:S(2)}) collective-permute-start(bf16[128,256]{1,0:T(8,128)(2,1)} %get-tuple-element.40), channel_id=1, source_target_pairs={{0,24},{1,25},{2,26},{3,27},{4,28},{5,29},{6,30},{7,31},{8,0},{9,1... | collective-permute-start | bytes 196616 | tf_op jit(solution)/shard_map/spread_keys/ppermute | solution.py:54
  8.9 0.0 copy-start
  8.9 1.2 %copy-done = bf16[128,4096]{1,0:T(8,128)(2,1)S(1)} copy-done((bf16[128,4096]{1,0:T(8,128)(2,1)S(1)}, bf16[128,4096]{1,0:T(8,128)(2,1)}, u32[]{:S(2)}) %copy-start) | copy-done | bytes 1048600
  10.1 0.0 copy-start.1
  10.1 1.2 %copy-done.1 = bf16[128,4096]{1,0:T(8,128)(2,1)S(1)} copy-done((bf16[128,4096]{1,0:T(8,128)(2,1)S(1)}, bf16[128,4096]{1,0:T(8,128)(2,1)}, u32[]{:S(2)}) %copy-start.1) | copy-done | bytes 1048600
  11.3 0.2 pack.3
  11.6 0.0 collective-permute-done
  11.6 0.0 collective-permute-done.1
  11.6 0.7 collective-permute-done.2
  12.3 0.4 collective-permute-start.3
  12.7 2.9 %collective-permute-start.4 = (bf16[128,2048]{1,0:T(8,128)(2,1)S(1)}, bf16[128,2048]{1,0:T(8,128)(2,1)S(1)}, u32[]{:S(2)}, u32[]{:S(2)}) collective-permute-start(bf16[128,2048]{1,0:T(8,128)(2,1)S(1)} %get-tuple-element.47), channel_id=1, source_target_pairs={{0,24},{1,25},{2,26},{3,27},{4,28},{5,29},{6,30},{7,31},{8,0},{9,1... | collective-permute-start | bytes 1572872 | tf_op jit(solution)/shard_map/spread_queries/ppermute | solution.py:54
  15.6 0.0 copy-done.4
  15.6 3.1 %collective-permute-start.8 = (bf16[4,128,256]{2,1,0:T(8,128)(2,1)S(1)}, bf16[4,128,256]{2,1,0:T(8,128)(2,1)S(1)}, u32[]{:S(2)}, u32[]{:S(2)}) collective-permute-start(bf16[4,128,256]{2,1,0:T(8,128)(2,1)S(1)} %pad_maximum_fusion.refs_3_), channel_id=1, source_target_pairs={{0,6},{1,7},{2,0},{3,1},{4,2},{5,3},{6,4},{7,5},{8,14},{9,15},{10,... | collective-permute-start | bytes 786440 | tf_op jit(solution)/shard_map/spread_keys/ppermute | solution.py:54
  18.7 0.6 collective-permute-start.7
  19.3 1.0 %collective-permute-start.6 = (bf16[4,128,256]{2,1,0:T(8,128)(2,1)S(1)}, bf16[4,128,256]{2,1,0:T(8,128)(2,1)S(1)}, u32[]{:S(2)}, u32[]{:S(2)}) collective-permute-start(bf16[4,128,256]{2,1,0:T(8,128)(2,1)S(1)} %pad_maximum_fusion.refs_3_), channel_id=1, source_target_pairs={{0,2},{1,3},{2,4},{3,5},{4,6},{5,7},{6,0},{7,1},{8,10},{9,11},{10,... | collective-permute-start | bytes 786440 | tf_op jit(solution)/shard_map/spread_keys/ppermute | solution.py:54
  20.3 7.6 %collective-permute-done.8.refs_6_ = bf16[4,128,256]{2,1,0:T(8,128)(2,1)S(1)} collective-permute-done((bf16[4,128,256]{2,1,0:T(8,128)(2,1)S(1)}, bf16[4,128,256]{2,1,0:T(8,128)(2,1)S(1)}, u32[]{:S(2)}, u32[]{:S(2)}) %collective-permute-start.8) | collective-permute-done | bytes 262176 | tf_op jit(solution)/shard_map/spread_keys/ppermute | solution.py:54
  27.9 0.0 collective-permute-start.9
  27.9 1.0 %collective-permute-done.7.refs_5_ = bf16[4,128,256]{2,1,0:T(8,128)(2,1)S(1)} collective-permute-done((bf16[4,128,256]{2,1,0:T(8,128)(2,1)S(1)}, bf16[4,128,256]{2,1,0:T(8,128)(2,1)S(1)}, u32[]{:S(2)}, u32[]{:S(2)}) %collective-permute-start.7) | collective-permute-done | bytes 262176 | tf_op jit(solution)/shard_map/spread_keys/ppermute | solution.py:54
  28.9 0.0 collective-permute-start.12
  28.9 2.7 %collective-permute-done.6.refs_4_ = bf16[4,128,256]{2,1,0:T(8,128)(2,1)S(1)} collective-permute-done((bf16[4,128,256]{2,1,0:T(8,128)(2,1)S(1)}, bf16[4,128,256]{2,1,0:T(8,128)(2,1)S(1)}, u32[]{:S(2)}, u32[]{:S(2)}) %collective-permute-start.6) | collective-permute-done | bytes 262176 | tf_op jit(solution)/shard_map/spread_keys/ppermute | solution.py:54
  31.6 0.0 collective-permute-start.11
  31.6 0.0 collective-permute-done.3.refs_1_
  31.6 0.5 collective-permute-start.10
  32.1 0.0 collective-permute-done.4.refs_2_
  32.1 0.7 collective-permute-start.5
  32.9 0.0 collective-permute-done.9.refs_7_
  32.9 0.0 collective-permute-done.12.refs_10_
  32.9 0.3 collective-permute-done.11.refs_9_
  33.2 0.4 collective-permute-done.10.refs_8_
  33.5 0.0 copy-done.2
  33.5 0.0 copy-done.3
  33.5 13.4 %attention_first.1 = (bf16[128,1024]{1,0:T(8,128)(2,1)S(1)}, bf16[128,1024]{1,0:T(8,128)(2,1)S(1)}, bf16[128,1024]{1,0:T(8,128)(2,1)S(1)}, bf16[4096,128]{1,0:T(...) custom-call(s32[32]{0:T(128)S(1)} %copy-done.2, s32[8]{0:T(128)S(1)} %copy-done.3, ...), custom_call_target="tpu_custom_call" | custom-call | flops 4026531840 | bytes 8388608 | tf_op jit(solution)/shard_map/attention/attention_first/pallas_call | solution.py:362
  46.9 0.7 collective-permute-done.5.refs_0_
  47.6 2.9 %attention_last.1 = (bf16[128,1024]{1,0:T(8,128)(2,1)S(1)}, bf16[4,4,128,256]{3,2,1,0:T(8,128)(2,1)S(1)}, bf16[4,4,128,256]{3,2,1,0:T(8,128)(2,1)S(1)}) custom-call(s32[32]{0:T(128)S(1)} %copy-done.2, s32[8]{0:T(128)S(1)} %copy-done.3, bf16[128,2048]{1,0:T(8,128)(2,1)S(1)} %collective-permute-done.5.refs_0_, ...), custom_call_target="tpu_custom_call" | custom-call | flops 1342177280 | bytes 8388608 | tf_op jit(solution)/shard_map/attention/attention_last/pallas_call | solution.py:379
  50.5 8.8 %collective-permute-start.13 = (bf16[4,4,128,256]{3,2,1,0:T(8,128)(2,1)S(1)}, bf16[4,4,128,256]{3,2,1,0:T(8,128)(2,1)S(1)}, u32[]{:S(2)}, u32[]{:S(2)}) collective-permute-start(bf16[4,4,128,256]{3,2,1,0:T(8,128)(2,1)S(1)} %get-tuple-element.61), channel_id=1, source_target_pairs={{0,1},{1,0},{2,3},{3,2},{4,5},{5,4},{6,7},{7,6},{8,9},{9,8},{10,11... | collective-permute-start | bytes 3145736 | tf_op jit(solution)/shard_map/return_keys/ppermute | solution.py:54
  59.3 1.0 %collective-permute-start.17 = (bf16[128,1024]{1,0:T(8,128)(2,1)S(1)}, bf16[128,1024]{1,0:T(8,128)(2,1)S(1)}, u32[]{:S(2)}, u32[]{:S(2)}) collective-permute-start(bf16[128,1024]{1,0:T(8,128)(2,1)S(1)} %get-tuple-element.64), channel_id=1, source_target_pairs={{0,24},{1,25},{2,26},{3,27},{4,28},{5,29},{6,30},{7,31},{8,0},{9,1... | collective-permute-start | bytes 786440 | tf_op jit(solution)/shard_map/return_keys/ppermute | solution.py:54
  60.3 1.3 %collective-permute-start.18 = (bf16[128,1024]{1,0:T(8,128)(2,1)S(1)}, bf16[128,1024]{1,0:T(8,128)(2,1)S(1)}, u32[]{:S(2)}, u32[]{:S(2)}) collective-permute-start(bf16[128,1024]{1,0:T(8,128)(2,1)S(1)} %get-tuple-element.65), channel_id=1, source_target_pairs={{0,16},{1,17},{2,18},{3,19},{4,20},{5,21},{6,22},{7,23},{8,24},{9,... | collective-permute-start | bytes 786440 | tf_op jit(solution)/shard_map/return_keys/ppermute | solution.py:54
  61.6 0.0 collective-permute-done.13
  61.6 0.4 add_convert_fusion
  62.0 0.1 slice_bitcast_fusion
  62.0 0.1 collective-permute-start.16
  62.1 0.1 collective-permute-start.15
  62.2 1.9 %collective-permute-start.14 = (bf16[4,128,256]{2,1,0:T(8,128)(2,1)S(1)}, bf16[4,128,256]{2,1,0:T(8,128)(2,1)S(1)}, u32[]{:S(2)}, u32[]{:S(2)}) collective-permute-start(bf16[4,128,256]{2,1,0:T(8,128)(2,1)S(1)} %get-tuple-element.73), channel_id=1, source_target_pairs={{0,2},{1,3},{2,4},{3,5},{4,6},{5,7},{6,0},{7,1},{8,10},{9,11},{10,... | collective-permute-start | bytes 786440 | tf_op jit(solution)/shard_map/return_keys/ppermute | solution.py:54
  64.1 4.3 %collective-permute-done.17.dq1 = bf16[128,1024]{1,0:T(8,128)(2,1)S(1)} collective-permute-done((bf16[128,1024]{1,0:T(8,128)(2,1)S(1)}, bf16[128,1024]{1,0:T(8,128)(2,1)S(1)}, u32[]{:S(2)}, u32[]{:S(2)}) %collective-permute-start.17) | collective-permute-done | bytes 262176 | tf_op jit(solution)/shard_map/return_keys/ppermute | solution.py:54
  68.5 1.3 %collective-permute-done.18.dq2 = bf16[128,1024]{1,0:T(8,128)(2,1)S(1)} collective-permute-done((bf16[128,1024]{1,0:T(8,128)(2,1)S(1)}, bf16[128,1024]{1,0:T(8,128)(2,1)S(1)}, u32[]{:S(2)}, u32[]{:S(2)}) %collective-permute-start.18) | collective-permute-done | bytes 262176 | tf_op jit(solution)/shard_map/return_keys/ppermute | solution.py:54
  69.8 1.2 %join_early.1.grad_in = f32[128,4096]{1,0:T(8,128)} custom-call(bf16[128,1024]{1,0:T(8,128)(2,1)S(1)} %get-tuple-element.63.dq0, bf16[128,1024]{1,0:T(8,128)(2,1)S(1)} %collective-permute-done.17.dq1, bf16[128,1024]{1,0:T(8,128)(2,1)S(1)} %collective-permute-done.18.dq2), custom_call_target="tpu_custom_call" | custom-call | bytes 3145728 | tf_op jit(solution)/shard_map/return_keys/join_early/pallas_call | solution.py:113
  71.0 0.2 collective-permute-done.16
  71.2 1.6 %collective-permute-done.15 = bf16[4,128,256]{2,1,0:T(8,128)(2,1)S(1)} collective-permute-done((bf16[4,128,256]{2,1,0:T(8,128)(2,1)S(1)}, bf16[4,128,256]{2,1,0:T(8,128)(2,1)S(1)}, u32[]{:S(2)}, u32[]{:S(2)}) %collective-permute-start.15) | collective-permute-done | bytes 262176 | tf_op jit(solution)/shard_map/return_keys/ppermute | solution.py:54
  72.9 5.0 %collective-permute-done.14 = bf16[4,128,256]{2,1,0:T(8,128)(2,1)S(1)} collective-permute-done((bf16[4,128,256]{2,1,0:T(8,128)(2,1)S(1)}, bf16[4,128,256]{2,1,0:T(8,128)(2,1)S(1)}, u32[]{:S(2)}, u32[]{:S(2)}) %collective-permute-start.14) | collective-permute-done | bytes 262176 | tf_op jit(solution)/shard_map/return_keys/ppermute | solution.py:54
  77.9 0.2 collective-permute-start.22
  78.1 0.1 fusion.2
  78.3 3.1 %collective-permute-start.21 = (bf16[128,256]{1,0:T(8,128)(2,1)S(1)}, bf16[128,256]{1,0:T(8,128)(2,1)S(1)}, u32[]{:S(2)}, u32[]{:S(2)}) collective-permute-start(bf16[128,256]{1,0:T(8,128)(2,1)S(1)} %get-tuple-element.74), channel_id=1, source_target_pairs={{0,24},{1,25},{2,26},{3,27},{4,28},{5,29},{6,30},{7,31},{8,0},{9,1... | collective-permute-start | bytes 196616 | tf_op jit(solution)/shard_map/return_keys/ppermute | solution.py:54
  81.4 0.6 collective-permute-start.20
  82.0 0.6 collective-permute-start.19
  82.6 1.5 %collective-permute-done.21.part3 = bf16[128,256]{1,0:T(8,128)(2,1)S(1)} collective-permute-done((bf16[128,256]{1,0:T(8,128)(2,1)S(1)}, bf16[128,256]{1,0:T(8,128)(2,1)S(1)}, u32[]{:S(2)}, u32[]{:S(2)}) %collective-permute-start.21) | collective-permute-done | bytes 65568 | tf_op jit(solution)/shard_map/return_keys/ppermute | solution.py:54
  84.1 5.3 %collective-permute-done.20.part2 = bf16[128,256]{1,0:T(8,128)(2,1)S(1)} collective-permute-done((bf16[128,256]{1,0:T(8,128)(2,1)S(1)}, bf16[128,256]{1,0:T(8,128)(2,1)S(1)}, u32[]{:S(2)}, u32[]{:S(2)}) %collective-permute-start.20) | collective-permute-done | bytes 65568 | tf_op jit(solution)/shard_map/return_keys/ppermute | solution.py:54
  89.3 0.8 collective-permute-done.19.part1
  90.2 0.0 collective-permute-done.22.dq3
  90.2 1.6 %finish.1 = (f32[128,4096]{1,0:T(8,128)}, f32[128,512]{1,0:T(8,128)}, f32[128,512]{1,0:T(8,128)}) custom-call(bf16[128,256]{1,0:T(8,128)(2,1)S(1)} %get-tuple-element.77.part0, bf16[128,256]{1,0:T(8,128)(2,1)S(1)} %collective-permute-done.19.part1, bf16[128,256]{1,0:T(8,128)(2,1)S(1)} %collective-permute-done.20.part2, ...), custom_call_target="tpu_custom_call", output_to_operand_aliasing={{0}: (5, {})} | custom-call | bytes 4194304 | tf_op jit(solution)/shard_map/return_keys/finish/pallas_call | solution.py:139
  (3 shorter events, 0.1 us)
Async XLA Ops:
  0.6 32.9 %copy-start.2 = (s32[32]{0:T(128)S(1)}, s32[32]{0:T(128)}, u32[]{:S(2)}) copy-start(s32[32]{0:T(128)} %plan.3) | copy-start | bytes 388
  0.6 32.9 %copy-start.3 = (s32[8]{0:T(128)S(1)}, s32[8]{0:T(128)}, u32[]{:S(2)}) copy-start(s32[8]{0:T(128)} %lengths.3) | copy-start | bytes 100
  2.3 9.3 %collective-permute-start = (bf16[128,256]{1,0:T(8,128)(2,1)}, bf16[128,256]{1,0:T(8,128)(2,1)S(1)}, u32[]{:S(2)}, u32[]{:S(2)}) collective-permute-start(bf16[128,256]{1,0:T(8,128)(2,1)} %get-tuple-element.38), channel_id=1, source_target_pairs={{0,8},{1,9},{2,10},{3,11},{4,12},{5,13},{6,14},{7,15},{8,16},{9,17... | collective-permute-start | bytes 196616 | tf_op jit(solution)/shard_map/spread_keys/ppermute | solution.py:54
  4.3 7.3 %collective-permute-start.1 = (bf16[128,256]{1,0:T(8,128)(2,1)}, bf16[128,256]{1,0:T(8,128)(2,1)S(1)}, u32[]{:S(2)}, u32[]{:S(2)}) collective-permute-start(bf16[128,256]{1,0:T(8,128)(2,1)} %get-tuple-element.39), channel_id=1, source_target_pairs={{0,16},{1,17},{2,18},{3,19},{4,20},{5,21},{6,22},{7,23},{8,24},{9,... | collective-permute-start | bytes 196616 | tf_op jit(solution)/shard_map/spread_keys/ppermute | solution.py:54
  7.9 4.5 %collective-permute-start.2 = (bf16[128,256]{1,0:T(8,128)(2,1)}, bf16[128,256]{1,0:T(8,128)(2,1)S(1)}, u32[]{:S(2)}, u32[]{:S(2)}) collective-permute-start(bf16[128,256]{1,0:T(8,128)(2,1)} %get-tuple-element.40), channel_id=1, source_target_pairs={{0,24},{1,25},{2,26},{3,27},{4,28},{5,29},{6,30},{7,31},{8,0},{9,1... | collective-permute-start | bytes 196616 | tf_op jit(solution)/shard_map/spread_keys/ppermute | solution.py:54
  8.9 1.2 %copy-start = (bf16[128,4096]{1,0:T(8,128)(2,1)S(1)}, bf16[128,4096]{1,0:T(8,128)(2,1)}, u32[]{:S(2)}) copy-start(bf16[128,4096]{1,0:T(8,128)(2,1)} %left.3) | copy-start | bytes 3145732
  10.1 1.2 %copy-start.1 = (bf16[128,4096]{1,0:T(8,128)(2,1)S(1)}, bf16[128,4096]{1,0:T(8,128)(2,1)}, u32[]{:S(2)}) copy-start(bf16[128,4096]{1,0:T(8,128)(2,1)} %right.3) | copy-start | bytes 3145732
  11.3 4.3 %copy-start.4 = (bf16[128,256]{1,0:T(8,128)(2,1)S(1)}, bf16[128,256]{1,0:T(8,128)(2,1)}, u32[]{:S(2)}) copy-start(bf16[128,256]{1,0:T(8,128)(2,1)} %get-tuple-element.52) | copy-start | bytes 196612
  12.3 19.3 %collective-permute-start.3 = (bf16[128,2048]{1,0:T(8,128)(2,1)S(1)}, bf16[128,2048]{1,0:T(8,128)(2,1)S(1)}, u32[]{:S(2)}, u32[]{:S(2)}) collective-permute-start(bf16[128,2048]{1,0:T(8,128)(2,1)S(1)} %get-tuple-element.46), channel_id=1, source_target_pairs={{0,8},{1,9},{2,10},{3,11},{4,12},{5,13},{6,14},{7,15},{8,16},{9,17... | collective-permute-start | bytes 1572872 | tf_op jit(solution)/shard_map/spread_queries/ppermute | solution.py:54
  12.7 19.4 %collective-permute-start.4 = (bf16[128,2048]{1,0:T(8,128)(2,1)S(1)}, bf16[128,2048]{1,0:T(8,128)(2,1)S(1)}, u32[]{:S(2)}, u32[]{:S(2)}) collective-permute-start(bf16[128,2048]{1,0:T(8,128)(2,1)S(1)} %get-tuple-element.47), channel_id=1, source_target_pairs={{0,24},{1,25},{2,26},{3,27},{4,28},{5,29},{6,30},{7,31},{8,0},{9,1... | collective-permute-start | bytes 1572872 | tf_op jit(solution)/shard_map/spread_queries/ppermute | solution.py:54
  15.6 12.3 %collective-permute-start.8 = (bf16[4,128,256]{2,1,0:T(8,128)(2,1)S(1)}, bf16[4,128,256]{2,1,0:T(8,128)(2,1)S(1)}, u32[]{:S(2)}, u32[]{:S(2)}) collective-permute-start(bf16[4,128,256]{2,1,0:T(8,128)(2,1)S(1)} %pad_maximum_fusion.refs_3_), channel_id=1, source_target_pairs={{0,6},{1,7},{2,0},{3,1},{4,2},{5,3},{6,4},{7,5},{8,14},{9,15},{10,... | collective-permute-start | bytes 786440 | tf_op jit(solution)/shard_map/spread_keys/ppermute | solution.py:54
  18.7 10.2 %collective-permute-start.7 = (bf16[4,128,256]{2,1,0:T(8,128)(2,1)S(1)}, bf16[4,128,256]{2,1,0:T(8,128)(2,1)S(1)}, u32[]{:S(2)}, u32[]{:S(2)}) collective-permute-start(bf16[4,128,256]{2,1,0:T(8,128)(2,1)S(1)} %pad_maximum_fusion.refs_3_), channel_id=1, source_target_pairs={{0,4},{1,5},{2,6},{3,7},{4,0},{5,1},{6,2},{7,3},{8,12},{9,13},{10,... | collective-permute-start | bytes 786440 | tf_op jit(solution)/shard_map/spread_keys/ppermute | solution.py:54
  19.3 12.3 %collective-permute-start.6 = (bf16[4,128,256]{2,1,0:T(8,128)(2,1)S(1)}, bf16[4,128,256]{2,1,0:T(8,128)(2,1)S(1)}, u32[]{:S(2)}, u32[]{:S(2)}) collective-permute-start(bf16[4,128,256]{2,1,0:T(8,128)(2,1)S(1)} %pad_maximum_fusion.refs_3_), channel_id=1, source_target_pairs={{0,2},{1,3},{2,4},{3,5},{4,6},{5,7},{6,0},{7,1},{8,10},{9,11},{10,... | collective-permute-start | bytes 786440 | tf_op jit(solution)/shard_map/spread_keys/ppermute | solution.py:54
  27.9 5.0 %collective-permute-start.9 = (bf16[4,128,256]{2,1,0:T(8,128)(2,1)S(1)}, bf16[4,128,256]{2,1,0:T(8,128)(2,1)S(1)}, u32[]{:S(2)}, u32[]{:S(2)}) collective-permute-start(bf16[4,128,256]{2,1,0:T(8,128)(2,1)S(1)} %pad_maximum_fusion.refs_3_), channel_id=1, source_target_pairs={{0,1},{1,0},{2,3},{3,2},{4,5},{5,4},{6,7},{7,6},{8,9},{9,8},{10,11... | collective-permute-start | bytes 786440 | tf_op jit(solution)/shard_map/spread_keys/ppermute | solution.py:54
  28.9 4.0 %collective-permute-start.12 = (bf16[4,128,256]{2,1,0:T(8,128)(2,1)S(1)}, bf16[4,128,256]{2,1,0:T(8,128)(2,1)S(1)}, u32[]{:S(2)}, u32[]{:S(2)}) collective-permute-start(bf16[4,128,256]{2,1,0:T(8,128)(2,1)S(1)} %collective-permute-done.8.refs_6_), channel_id=1, source_target_pairs={{0,1},{1,0},{2,3},{3,2},{4,5},{5,4},{6,7},{7,6},{8,9},{9,8},{10,11... | collective-permute-start | bytes 786440 | tf_op jit(solution)/shard_map/spread_keys/ppermute | solution.py:54
  31.6 1.5 %collective-permute-start.11 = (bf16[4,128,256]{2,1,0:T(8,128)(2,1)S(1)}, bf16[4,128,256]{2,1,0:T(8,128)(2,1)S(1)}, u32[]{:S(2)}, u32[]{:S(2)}) collective-permute-start(bf16[4,128,256]{2,1,0:T(8,128)(2,1)S(1)} %collective-permute-done.7.refs_5_), channel_id=1, source_target_pairs={{0,1},{1,0},{2,3},{3,2},{4,5},{5,4},{6,7},{7,6},{8,9},{9,8},{10,11... | collective-permute-start | bytes 786440 | tf_op jit(solution)/shard_map/spread_keys/ppermute | solution.py:54
  31.6 1.9 %collective-permute-start.10 = (bf16[4,128,256]{2,1,0:T(8,128)(2,1)S(1)}, bf16[4,128,256]{2,1,0:T(8,128)(2,1)S(1)}, u32[]{:S(2)}, u32[]{:S(2)}) collective-permute-start(bf16[4,128,256]{2,1,0:T(8,128)(2,1)S(1)} %collective-permute-done.6.refs_4_), channel_id=1, source_target_pairs={{0,1},{1,0},{2,3},{3,2},{4,5},{5,4},{6,7},{7,6},{8,9},{9,8},{10,11... | collective-permute-start | bytes 786440 | tf_op jit(solution)/shard_map/spread_keys/ppermute | solution.py:54
  32.1 15.4 %collective-permute-start.5 = (bf16[128,2048]{1,0:T(8,128)(2,1)S(1)}, bf16[128,2048]{1,0:T(8,128)(2,1)S(1)}, u32[]{:S(2)}, u32[]{:S(2)}) collective-permute-start(bf16[128,2048]{1,0:T(8,128)(2,1)S(1)} %get-tuple-element.48), channel_id=1, source_target_pairs={{0,16},{1,17},{2,18},{3,19},{4,20},{5,21},{6,22},{7,23},{8,24},{9,... | collective-permute-start | bytes 1572872 | tf_op jit(solution)/shard_map/spread_queries/ppermute | solution.py:54
  50.5 11.1 %collective-permute-start.13 = (bf16[4,4,128,256]{3,2,1,0:T(8,128)(2,1)S(1)}, bf16[4,4,128,256]{3,2,1,0:T(8,128)(2,1)S(1)}, u32[]{:S(2)}, u32[]{:S(2)}) collective-permute-start(bf16[4,4,128,256]{3,2,1,0:T(8,128)(2,1)S(1)} %get-tuple-element.61), channel_id=1, source_target_pairs={{0,1},{1,0},{2,3},{3,2},{4,5},{5,4},{6,7},{7,6},{8,9},{9,8},{10,11... | collective-permute-start | bytes 3145736 | tf_op jit(solution)/shard_map/return_keys/ppermute | solution.py:54
  59.3 9.2 %collective-permute-start.17 = (bf16[128,1024]{1,0:T(8,128)(2,1)S(1)}, bf16[128,1024]{1,0:T(8,128)(2,1)S(1)}, u32[]{:S(2)}, u32[]{:S(2)}) collective-permute-start(bf16[128,1024]{1,0:T(8,128)(2,1)S(1)} %get-tuple-element.64), channel_id=1, source_target_pairs={{0,24},{1,25},{2,26},{3,27},{4,28},{5,29},{6,30},{7,31},{8,0},{9,1... | collective-permute-start | bytes 786440 | tf_op jit(solution)/shard_map/return_keys/ppermute | solution.py:54
  60.3 9.5 %collective-permute-start.18 = (bf16[128,1024]{1,0:T(8,128)(2,1)S(1)}, bf16[128,1024]{1,0:T(8,128)(2,1)S(1)}, u32[]{:S(2)}, u32[]{:S(2)}) collective-permute-start(bf16[128,1024]{1,0:T(8,128)(2,1)S(1)} %get-tuple-element.65), channel_id=1, source_target_pairs={{0,16},{1,17},{2,18},{3,19},{4,20},{5,21},{6,22},{7,23},{8,24},{9,... | collective-permute-start | bytes 786440 | tf_op jit(solution)/shard_map/return_keys/ppermute | solution.py:54
  62.0 9.2 %collective-permute-start.16 = (bf16[4,128,256]{2,1,0:T(8,128)(2,1)S(1)}, bf16[4,128,256]{2,1,0:T(8,128)(2,1)S(1)}, u32[]{:S(2)}, u32[]{:S(2)}) collective-permute-start(bf16[4,128,256]{2,1,0:T(8,128)(2,1)S(1)} %get-tuple-element.71), channel_id=1, source_target_pairs={{0,6},{1,7},{2,0},{3,1},{4,2},{5,3},{6,4},{7,5},{8,14},{9,15},{10,... | collective-permute-start | bytes 786440 | tf_op jit(solution)/shard_map/return_keys/ppermute | solution.py:54
  62.1 10.8 %collective-permute-start.15 = (bf16[4,128,256]{2,1,0:T(8,128)(2,1)S(1)}, bf16[4,128,256]{2,1,0:T(8,128)(2,1)S(1)}, u32[]{:S(2)}, u32[]{:S(2)}) collective-permute-start(bf16[4,128,256]{2,1,0:T(8,128)(2,1)S(1)} %get-tuple-element.72), channel_id=1, source_target_pairs={{0,4},{1,5},{2,6},{3,7},{4,0},{5,1},{6,2},{7,3},{8,12},{9,13},{10,... | collective-permute-start | bytes 786440 | tf_op jit(solution)/shard_map/return_keys/ppermute | solution.py:54
  62.2 15.7 %collective-permute-start.14 = (bf16[4,128,256]{2,1,0:T(8,128)(2,1)S(1)}, bf16[4,128,256]{2,1,0:T(8,128)(2,1)S(1)}, u32[]{:S(2)}, u32[]{:S(2)}) collective-permute-start(bf16[4,128,256]{2,1,0:T(8,128)(2,1)S(1)} %get-tuple-element.73), channel_id=1, source_target_pairs={{0,2},{1,3},{2,4},{3,5},{4,6},{5,7},{6,0},{7,1},{8,10},{9,11},{10,... | collective-permute-start | bytes 786440 | tf_op jit(solution)/shard_map/return_keys/ppermute | solution.py:54
  77.9 12.3 %collective-permute-start.22 = (bf16[128,1024]{1,0:T(8,128)(2,1)S(1)}, bf16[128,1024]{1,0:T(8,128)(2,1)S(1)}, u32[]{:S(2)}, u32[]{:S(2)}) collective-permute-start(bf16[128,1024]{1,0:T(8,128)(2,1)S(1)} %get-tuple-element.69), channel_id=1, source_target_pairs={{0,8},{1,9},{2,10},{3,11},{4,12},{5,13},{6,14},{7,15},{8,16},{9,17... | collective-permute-start | bytes 786440 | tf_op jit(solution)/shard_map/return_keys/ppermute | solution.py:54
  78.3 5.8 %collective-permute-start.21 = (bf16[128,256]{1,0:T(8,128)(2,1)S(1)}, bf16[128,256]{1,0:T(8,128)(2,1)S(1)}, u32[]{:S(2)}, u32[]{:S(2)}) collective-permute-start(bf16[128,256]{1,0:T(8,128)(2,1)S(1)} %get-tuple-element.74), channel_id=1, source_target_pairs={{0,24},{1,25},{2,26},{3,27},{4,28},{5,29},{6,30},{7,31},{8,0},{9,1... | collective-permute-start | bytes 196616 | tf_op jit(solution)/shard_map/return_keys/ppermute | solution.py:54
  81.4 8.0 %collective-permute-start.20 = (bf16[128,256]{1,0:T(8,128)(2,1)S(1)}, bf16[128,256]{1,0:T(8,128)(2,1)S(1)}, u32[]{:S(2)}, u32[]{:S(2)}) collective-permute-start(bf16[128,256]{1,0:T(8,128)(2,1)S(1)} %get-tuple-element.75), channel_id=1, source_target_pairs={{0,16},{1,17},{2,18},{3,19},{4,20},{5,21},{6,22},{7,23},{8,24},{9,... | collective-permute-start | bytes 196616 | tf_op jit(solution)/shard_map/return_keys/ppermute | solution.py:54
  82.0 8.2 %collective-permute-start.19 = (bf16[128,256]{1,0:T(8,128)(2,1)S(1)}, bf16[128,256]{1,0:T(8,128)(2,1)S(1)}, u32[]{:S(2)}, u32[]{:S(2)}) collective-permute-start(bf16[128,256]{1,0:T(8,128)(2,1)S(1)} %get-tuple-element.76), channel_id=1, source_target_pairs={{0,8},{1,9},{2,10},{3,11},{4,12},{5,13},{6,14},{7,15},{8,16},{9,17... | collective-permute-start | bytes 196616 | tf_op jit(solution)/shard_map/return_keys/ppermute | solution.py:54
